TPU v7x, 128 devices: a whole 4x4x4 slice. The times are simulated.
128 devices in a mesh: inner: 16 (over z, y), target: 8 (over x, core).
Axes of the slice: x: 4, y: 4, z: 4, core: 2. Of those that a mesh axis runs over, the one named last changes fastest.
Arguments:
- left_factors: float32 [64, 64, 1024, 64], P('target', 'inner'), may hold values from -6 to 6
- mid_factors: float32 [64, 64, 1024, 64], P('target', 'inner'), may hold values from -0.1875 to 0.1875
- row_factors: float32 [64, 1024, 64], P('inner'), may hold values from -6 to 6
- col_factors: float32 [64, 1024, 64], P('inner'), may hold values from -0.09375 to 0.09375
- lists: int32 [64, 64], P('target'), may hold values from -1 to 63, as said below
- sketch_right: float32 [1024, 128], replicated, may hold values from -0.046875 to 0.046875
- sketch_left: float32 [1024, 128], replicated, may hold values from -0.046875 to 0.046875
- diag_tile: float32 [1024, 1024], P(None, 'target'), as said below
Outputs:
- left_sketch: float32 [64, 1024, 128], P('target', 'inner')
- right_factor: float32 [64, 128, 1024], P('target', 'inner')
- core: float32 [64, 128, 128], P('target', 'inner')
Inputs may be any that keep to these rules, and one draw needn't show every extreme that they name: `lists`: row t holds each contributing inner index once in any order and -1 in the other slots; the contributing indices of a row are 0 to c - 1 for some count c of 1 to 64, and some row has all 64. `diag_tile`: upper triangular with diagonal entries of 1 to 2.
All inputs are finite; a program needn't handle non-finite values.
Results may differ from a plain program's by a relative error of at most 0.0003.
Values sent between devices are 32-bit elements; how exact they have to be, the bound alone decides.
A program may use at most 128 MiB of HBM per device.

v0:
```python
import jax
import jax.numpy as jnp
from jax import lax
from jax.sharding import PartitionSpec as P

precision_top = lax.Precision.HIGHEST


def block_inverses(full_tile):
    order = full_tile.shape[0]
    width = min(128, order)
    count = order // width
    blocks = jnp.stack(
        [full_tile[j * width : (j + 1) * width, j * width : (j + 1) * width] for j in range(count)]
    )
    eye_block = jnp.eye(width, dtype=jnp.float32)
    diag_vals = jnp.diagonal(blocks, axis1=1, axis2=2)
    strict_part = blocks / diag_vals[:, :, None] - eye_block[None, :, :]
    power = -strict_part
    product = eye_block[None, :, :] + power
    for level in range(width.bit_length() - 2):
        power = jnp.einsum("nij,njk->nik", power, power, precision=precision_top)
        product = jnp.einsum(
            "nij,njk->nik", product, eye_block[None, :, :] + power, precision=precision_top
        )
    return (product / diag_vals[:, None, :], width, count)


def upper_solve(full_tile, inverses, width, count, rhs_rows):
    pieces = []
    for j in range(count):
        target_cols = rhs_rows[:, j * width : (j + 1) * width]
        if j > 0:
            earlier = jnp.concatenate(pieces, axis=1)
            target_cols = target_cols - jnp.dot(
                earlier,
                full_tile[: j * width, j * width : (j + 1) * width],
                precision=precision_top,
            )
        pieces.append(jnp.dot(target_cols, inverses[j], precision=precision_top))
    return jnp.concatenate(pieces, axis=1)


def on_device(
    left_factors, mid_factors, row_factors, col_factors, lists, sketch_right, sketch_left, diag_tile
):
    local_count = row_factors.shape[0]
    first_index = lax.axis_index("inner") * local_count
    global_ids = first_index + jnp.arange(local_count, dtype=jnp.int32)
    present = jnp.sum((lists[:, :, None] == global_ids[None, None, :]).astype(jnp.float32), axis=1)
    coupling = (
        jnp.einsum("tkbr,kbq->tkrq", mid_factors, row_factors, precision=precision_top)
        * present[:, :, None, None]
    )
    col_sketch = jnp.einsum("kbr,bs->krs", col_factors, sketch_right, precision=precision_top)
    inner_left = jnp.einsum("tkrq,kqs->tkrs", coupling, col_sketch, precision=precision_top)
    left_part = jnp.einsum("tkbr,tkrs->tbs", left_factors, inner_left, precision=precision_top)
    projected = jnp.einsum("bs,tkbr->tksr", sketch_left, left_factors, precision=precision_top)
    joined = jnp.einsum("tksr,tkrq->tksq", projected, coupling, precision=precision_top)
    right_part = jnp.einsum("tksq,kbq->tsb", joined, col_factors, precision=precision_top)
    full_tile = lax.all_gather(diag_tile, "target", axis=1, tiled=True)
    tile_order = full_tile.shape[0]
    inverses, width, count = block_inverses(full_tile)
    left_rows, right_rows = (
        lax.psum_scatter(left_part, "inner", scatter_dimension=1, tiled=True),
        lax.psum_scatter(right_part, "inner", scatter_dimension=1, tiled=True),
    )
    core_rows = jnp.einsum("tsb,bq->tsq", right_rows, sketch_right, precision=precision_top)
    flat_rows = right_rows.reshape(-1, tile_order)
    solved = upper_solve(full_tile, inverses, width, count, flat_rows)
    solved_rows = solved.reshape(right_rows.shape)
    return (left_rows, solved_rows, core_rows)


def solution(mesh):
    placed = (
        P("target", "inner", None, None),
        P("target", "inner", None, None),
        P("inner", None, None),
        P("inner", None, None),
        P("target", None),
        P(),
        P(),
        P(None, "target"),
    )
    return jax.shard_map(
        on_device,
        mesh=mesh,
        in_specs=placed,
        out_specs=(
            P("target", "inner", None),
            P("target", "inner", None),
            P("target", "inner", None),
        ),
        check_vma=False,
    )
```

profile of v0, /device:TPU:0, one launch (start us, length us, event | category | flops | bytes accessed | tf_op | source)
XLA Modules:
  0.0 208.7 jit_solution(9203844053379159442)
XLA Ops:
  8.0 0.0 copy-start
  8.0 0.0 all-gather.2.cloned.1.call-start
  8.1 0.7 all-gather.2.cloned.1.call-update
  8.7 0.0 reduce-scatter.5.cloned.1.call-start
  8.8 0.8 convert_reduce_fusion
  9.7 10.0 %fusion.13 = f32[8,4,64,128]{3,2,1,0:T(8,128)S(1)} fusion(f32[8,4,1024,64]{2,3,1,0:T(8,128)} %param.8, f32[1024,128]{1,0:T(8,128)} %param.14), kind=kOutput, calls=%fused_computation.24 | convolution fusion | flops 3221225472 | bytes 9961472 | tf_op jit(solution)/shard_map/bs,tkbr->tksr/dot_general | solution.py:58
  19.7 0.0 copy-done.1
  19.7 0.0 copy-done.4
  19.7 12.2 %fusion.5 = f32[8,4,64,64]{2,3,0,1:T(8,128)S(1)} fusion(f32[8,4,1024,64]{2,3,1,0:T(8,128)S(1)} %copy-done.1, f32[4,1024,64]{1,2,0:T(8,128)S(1)} %copy-done.4, f32[8,4]{0,1:T(4,128)S(1)} %convert_reduce_fusion), kind=kOutput, calls=%fused_computation.7 | convolution fusion | flops 1610743808 | bytes 9961600 | tf_op jit(solution)/shard_map/tkbr,kbq->tkrq/dot_general | solution.py:52
  32.0 1.1 fusion.10
  33.1 0.0 copy-start.2
  33.1 5.1 %convolution_bitcast_fusion = f32[8,128,1024]{2,1,0:T(8,128)} fusion(f32[8,4,128,64]{2,3,1,0:T(8,128)S(1)} %fusion.10, f32[4,1024,64]{1,2,0:T(8,128)S(1)} %copy-done), kind=kOutput, calls=%fused_computation.3 | convolution fusion | flops 3221225472 | bytes 6291456 | tf_op jit(solution)/shard_map/tksq,kbq->tsb/dot_general | solution.py:60
  38.2 0.0 reduce-scatter.5.cloned.1.call-update
  38.3 0.2 reduce-scatter.3.cloned.1.call-start
  38.5 0.0 copy-done.2
  38.5 1.0 convolution_bitcast_fusion.3
  39.5 1.8 convolution_bitcast_fusion.2
  41.3 10.6 %convolution_bitcast_fusion.1 = f32[8,1024,128]{1,2,0:T(8,128)} fusion(f32[8,4,64,128]{3,2,1,0:T(8,128)S(1)} %convolution_bitcast_fusion.2, f32[8,4,1024,64]{2,3,1,0:T(8,128)} %param.8), kind=kOutput, calls=%fused_computation.4 | convolution fusion | flops 3221225472 | bytes 13631488 | tf_op jit(solution)/shard_map/tkbr,tkrs->tbs/dot_general | solution.py:57
  51.9 5.4 %copy.24 = f32[8,1024,128]{2,0,1:T(8,128)} copy(f32[8,1024,128]{1,2,0:T(8,128)} %convolution_bitcast_fusion.1) | data formatting | bytes 8388608 | tf_op jit(solution)/shard_map/tkbr,tkrs->tbs/dot_general | solution.py:57
  57.3 0.0 reduce-scatter.3.cloned.1.call-update
  57.3 0.0 all-gather.2.cloned.1.call-done
  57.4 0.8 constant_dynamic-update-slice_fusion.7
  58.2 0.8 constant_dynamic-update-slice_fusion.6
  59.1 0.8 constant_dynamic-update-slice_fusion.5
  59.9 0.8 constant_dynamic-update-slice_fusion.4
  60.8 0.8 constant_dynamic-update-slice_fusion.3
  61.6 0.8 constant_dynamic-update-slice_fusion.2
  62.4 0.8 constant_dynamic-update-slice_fusion.1
  63.3 0.8 constant_dynamic-update-slice_fusion
  64.1 4.8 %copy.26 = f32[8,128,128]{0,2,1:T(8,128)} copy(f32[8,128,128]{2,1,0:T(8,128)S(1)} %constant_dynamic-update-slice_fusion) | data formatting | bytes 1048576 | tf_op jit(solution)/shard_map/stack | solution.py:13
  68.9 1.8 gather_fusion
  70.8 0.9 fusion.39
  71.6 0.6 fusion.69
  72.3 0.6 fusion.70
  72.9 0.6 fusion.71
  73.5 0.6 fusion.72
  74.2 0.8 fusion.26
  74.9 0.6 fusion.24
  75.6 0.6 fusion.22
  76.3 0.6 fusion.20
  76.9 0.6 convolution_add_fusion
  77.5 0.6 fusion.18
  78.2 0.6 convolution_divide_fusion
  78.9 39.9 %reduce-scatter.5.cloned.1.call-done = f32[8,8,1024]{2,1,0:T(8,128)} async-done(((f32[8,128,1024]{2,1,0:T(8,128)}), f32[8,8,1024]{2,1,0:T(8,128)}) %reduce-scatter.5.cloned.1.call-update) | async-done | bytes 262160 | tf_op jit(solution)/shard_map/reduce_scatter | solution.py:66
  118.7 1.0 constant_dynamic-update-slice_fusion.25
  119.8 1.0 convolution_subtract_fusion.3
  120.8 0.2 constant_dynamic-update-slice_fusion.24
  121.0 1.1 convolution_subtract_fusion.2
  122.1 0.2 constant_dynamic-update-slice_fusion.23
  122.3 1.2 convolution_subtract_fusion.1
  123.5 0.2 constant_dynamic-update-slice_fusion.22
  123.7 1.2 convolution_subtract_fusion.6
  125.0 0.2 constant_dynamic-update-slice_fusion.21
  125.2 1.3 convolution_subtract_fusion.5
  126.5 0.2 constant_dynamic-update-slice_fusion.20
  126.7 1.4 convolution_subtract_fusion.4
  128.0 0.2 constant_dynamic-update-slice_fusion.19
  128.2 1.4 convolution_subtract_fusion
  129.7 0.2 convolution_dynamic-update-slice_fusion
  129.9 0.0 copy-start.5
  129.9 1.1 fusion.15
  130.9 68.4 %reduce-scatter.3.cloned.1.call-done = f32[8,64,128]{2,0,1:T(8,128)} async-done(((f32[8,1024,128]{2,0,1:T(8,128)}), f32[8,64,128]{2,0,1:T(8,128)}) %reduce-scatter.3.cloned.1.call-update) | async-done | bytes 262160 | tf_op jit(solution)/shard_map/reduce_scatter | solution.py:65
  199.4 1.7 copy.29
  201.1 0.0 copy-done.5
  (9 shorter events, 0.1 us)
Async XLA Ops:
  8.0 25.1 %copy-start = (f32[4,1024,64]{1,2,0:T(8,128)S(1)}, f32[4,1024,64]{1,2,0:T(8,128)}, u32[]{:S(2)}) copy-start(f32[4,1024,64]{1,2,0:T(8,128)} %param.11) | copy-start | bytes 3145732
  8.0 49.4 %all-gather.2.cloned.1.call-start = ((), (), s32[]{:S(2)}) async-start(), calls=%async_computation.4 | async-start | bytes 4718592 | tf_op jit(solution)/shard_map/all_gather | solution.py:61
  8.7 110.0 %reduce-scatter.5.cloned.1.call-start = ((), (), s32[]{:S(2)}) async-start(), calls=%async_computation.3 | async-start | bytes 4456448 | tf_op jit(solution)/shard_map/reduce_scatter | solution.py:66
  9.7 10.1 %copy-start.1 = (f32[8,4,1024,64]{2,3,1,0:T(8,128)S(1)}, f32[8,4,1024,64]{2,3,1,0:T(8,128)}, u32[]{:S(2)}) copy-start(f32[8,4,1024,64]{2,3,1,0:T(8,128)} %param.9) | copy-start | bytes 25165828
  9.7 10.1 %copy-start.4 = (f32[4,1024,64]{1,2,0:T(8,128)S(1)}, f32[4,1024,64]{1,2,0:T(8,128)}, u32[]{:S(2)}) copy-start(f32[4,1024,64]{1,2,0:T(8,128)} %param.10) | copy-start | bytes 3145732
  33.1 5.4 %copy-start.2 = (f32[1024,128]{1,0:T(8,128)S(1)}, f32[1024,128]{1,0:T(8,128)}, u32[]{:S(2)}) copy-start(f32[1024,128]{1,0:T(8,128)} %param.13) | copy-start | bytes 1572868
  38.3 161.1 %reduce-scatter.3.cloned.1.call-start = ((), (), s32[]{:S(2)}) async-start(), calls=%async_computation.2 | async-start | bytes 4456448 | tf_op jit(solution)/shard_map/reduce_scatter | solution.py:65
  118.7 11.1 %copy-start.3 = (f32[8,8,1024]{2,1,0:T(8,128)S(1)}, f32[8,8,1024]{2,1,0:T(8,128)}, u32[]{:S(2)}) copy-start(f32[8,8,1024]{2,1,0:T(8,128)} %reduce-scatter.5.cloned.1.call-done) | copy-start | bytes 786436
  129.9 71.2 %copy-start.5 = (f32[64,1024]{1,0:T(8,128)}, f32[64,1024]{1,0:T(8,128)S(1)}, u32[]{:S(2)}) copy-start(f32[64,1024]{1,0:T(8,128)S(1)} %convolution_dynamic-update-slice_fusion) | copy-start | bytes 786436
Sparse Core Ops, SparseCore 0:
  10.5 38.4 all-gather.1
Sparse Core Ops, SparseCore 1:
  38.4 80.3 reduce-scatter.4
  122.3 77.0 reduce-scatter.2
where the time goes:
time: 213 us; the launch traced here: 209 us
  waiting for transfers between devices  109 us (51%)
  matrix products  62 us (29%)
  local copies, waits for them, and re-layouts  20.5 us (10%)
  between operations  16 us (8%)
    reduce_scatter x1, waiting for transfers between devices, on_device(): lax.psum_scatter(left_part, 'inner', scatter_dimension=1, tiled=True)  68.4 us
    reduce_scatter x1, waiting for transfers between devices, on_device(): lax.psum_scatter(right_part, 'inner', scatter_dimension=1, tiled=True)  39.9 us
    dot_general x1, matrix products, on_device(): jnp.einsum('tkbr,kbq->tkrq', mid_factors, row_factors, precision=precisio...  12.2 us
    dot_general x1, matrix products, on_device(): jnp.einsum('tkbr,tkrs->tbs', left_factors, inner_left, precision=precisio...  10.6 us
    dot_general x1, matrix products, on_device(): jnp.einsum('bs,tkbr->tksr', sketch_left, left_factors, precision=precisio...  10 us
    dot_general x7, matrix products, upper_solve(): jnp.dot(earlier, full_tile[:j * width, j * width:(j + 1) * width], precis...  8.68 us
    unnamed x20, local copies, waits for them, and re-layouts  7.65 us
    another operation x2, local copies, waits for them, and re-layouts, block_inverses(): jnp.stack([full_tile[j * width:(j + 1) * width, j * width:(j + 1) * width...  5.64 us
  transfers between devices with their start and end apart: 3, of which 2 were waited for; matrix products, arithmetic and copies ran while one was open for 39% of the time, Pallas kernels for 0%

commit v1 on v0

v1 whole, which is shorter than its diff:
```python
import functools

import jax
import jax.numpy as jnp
from jax import lax
from jax.experimental import pallas as pl
from jax.experimental.pallas import tpu as pltpu
from jax.sharding import PartitionSpec as P

F32 = jnp.float32
BF16 = jnp.bfloat16
MESH = pl.DeviceIdType.MESH
NN = ((1,), (0,))
NT = ((1,), (1,))
SIDE = 4
UNITS = 16


def split(value):
    high = value.astype(BF16)
    return high, (value - high.astype(F32)).astype(BF16)


def mm(a, b, dims):
    return lax.dot_general(a, b, (dims, ((), ())), preferred_element_type=F32)


def mm3(a, b, dims):
    return mm(a[0], b[0], dims) + (mm(a[1], b[0], dims) + mm(a[0], b[1], dims))


def mm_top(a, b):
    return lax.dot_general(
        a, b, (NN, ((), ())), precision=lax.Precision.HIGHEST, preferred_element_type=F32
    )


def kernel(
    lt_hbm, mt_hbm, rt_hbm, ct_hbm, lists, om_hbm, psi_hbm, d_hbm,
    left_out, rf_out, core_out,
    lt, mt, rt, ct, om, psi, dfull, dinv, part, half, far1, near1, far2, near2,
    rts, psts, cols, ms, ls, cs, js, ws, doms,
    in_sem, send_sem, recv_sem, gs_sem, gr_sem,
):
    inner = lax.axis_index("inner")
    target = lax.axis_index("target")
    z, y = inner // SIDE, lax.rem(inner, SIDE)
    x, core = target // 2, lax.rem(target, 2)

    def turn(v, step):
        return lax.rem(v + step, SIDE)

    z_next = (turn(z, 1) * SIDE + y, turn(z, 3) * SIDE + y)
    y_next = (z * SIDE + turn(y, 1), z * SIDE + turn(y, 3))
    x_next = (turn(x, 1) * 2 + core, turn(x, 3) * 2 + core)
    sibling = x * 2 + (1 - core)

    loads = []

    def load(src, dst):
        copy = pltpu.make_async_copy(src, dst, in_sem.at[len(loads)])
        copy.start()
        loads.append(copy)
        return copy

    rt_load = load(rt_hbm, rt)
    ct_load = load(ct_hbm, ct)
    om_load = load(om_hbm, om)
    d_load = load(d_hbm, dfull.at[target])
    psi_load = load(psi_hbm, psi)
    in_base = 8

    def mt_copy(t):
        return pltpu.make_async_copy(mt_hbm.at[t], mt.at[t], in_sem.at[in_base + t])

    def lt_copy(t):
        return pltpu.make_async_copy(lt_hbm.at[t], lt.at[t], in_sem.at[in_base + 8 + t])

    @pl.loop(0, 8)
    def _(t):
        mt_copy(t).start()
        lt_copy(t).start()

    barrier = pltpu.get_barrier_semaphore()
    for peer in z_next + y_next:
        pl.semaphore_signal(barrier, inc=1, device_id=(peer, target), device_id_type=MESH)
    for peer in x_next + (sibling,):
        pl.semaphore_signal(barrier, inc=1, device_id=(inner, peer), device_id_type=MESH)
    pl.semaphore_wait(barrier, 7)

    def g_copy(src, dst, sem, peer):
        return pltpu.make_async_remote_copy(
            src_ref=src, dst_ref=dst, send_sem=gs_sem.at[sem], recv_sem=gr_sem.at[sem],
            device_id=(inner, peer), device_id_type=MESH,
        )

    def x_at(step, which):
        return turn(x, step) * 2 + which

    def gather_first(src, dst, base):
        for sem, peer in ((0, x_next[0]), (1, x_next[1]), (4, sibling)):
            g_copy(src, dst.at[target], base + sem, peer).start()

    def gather_second(dst, base, rows):
        before, after = dst.at[x_at(3, core)], dst.at[x_at(1, core)]
        g_copy(before, before, base + 0, sibling).wait_recv()
        g_copy(after, after, base + 1, sibling).wait_recv()
        low, top = before.at[pl.ds(0, rows)], after.at[pl.ds(rows, rows)]
        g_copy(low, low, base + 2, x_next[0]).start()
        g_copy(top, top, base + 3, x_next[1]).start()
        g_copy(before, before, base + 5, sibling).start()
        g_copy(after, after, base + 6, sibling).start()

    def gather_third(dst, base, rows):
        away = dst.at[x_at(2, core)]
        low, top = away.at[pl.ds(0, rows)], away.at[pl.ds(rows, rows)]
        g_copy(low, low, base + 2, sibling).wait_recv()
        g_copy(top, top, base + 3, sibling).wait_recv()
        g_copy(away, away, base + 7, sibling).start()

    def gather_last(dst, base):
        for sem, step in ((4, 0), (5, 3), (6, 1), (7, 2)):
            block = dst.at[x_at(step, 1 - core)]
            g_copy(block, block, base + sem, sibling).wait_recv()

    def gather_sent(src, dst, base, rows):
        for sem in (0, 1, 4, 5, 6, 7):
            g_copy(dst.at[0], dst.at[0], base + sem, sibling).wait_send()
        for sem in (2, 3):
            piece = dst.at[0, pl.ds(0, rows)]
            g_copy(piece, piece, base + sem, sibling).wait_send()

    gather_first(d_hbm, dfull, 0)

    def place(u, stage):
        axis = lax.rem(u + stage, 2)
        pos = z + axis * (y - z)
        peers = tuple(a + axis * (b - a) for a, b in zip(z_next, y_next))
        return pos, peers

    bufs = ((part, far1, near1, 2), (half, far2, near2, 1))

    def r_copy(stage, u, sem, src, dst, peer):
        return pltpu.make_async_remote_copy(
            src_ref=src, dst_ref=dst,
            send_sem=send_sem.at[stage, u, sem], recv_sem=recv_sem.at[stage, u, sem],
            device_id=(peer, target), device_id_type=MESH,
        )

    def piece(stage, u, chunk, h):
        buf, _, _, w = bufs[stage]
        return buf.at[u, pl.ds((2 * chunk + h) * w, w)]

    def start(stage, u):
        pos, peers = place(u, stage)
        _, far, near, _ = bufs[stage]
        for d in (0, 1):
            r_copy(stage, u, d, piece(stage, u, turn(pos, 2), d), far.at[u, d], peers[d]).start()
        for d in (0, 1):
            r_copy(
                stage, u, 2 + d, piece(stage, u, turn(pos, 1 + 2 * d), 1 - d),
                near.at[u, d, 1 - d], peers[d],
            ).start()

    def middle(stage, u):
        pos, peers = place(u, stage)
        _, far, near, _ = bufs[stage]
        for d in (0, 1):
            own = piece(stage, u, turn(pos, 1 + 2 * d), d)
            r_copy(stage, u, d, far.at[u, d], far.at[u, d], peers[d]).wait_recv()
            own[...] += far[u, d]
            r_copy(stage, u, 4 + d, own, near.at[u, d, d], peers[d]).start()

    def finish(stage, u):
        pos, peers = place(u, stage)
        _, far, near, _ = bufs[stage]
        for d in (0, 1):
            for h in (0, 1):
                sem = 4 + d if h == d else 2 + d
                r_copy(stage, u, sem, near.at[u, d, h], near.at[u, d, h], peers[d]).wait_recv()
        return [
            piece(stage, u, pos, h)[...] + near[u, 0, h] + near[u, 1, h] for h in (0, 1)
        ]

    def sent(stage, u):
        _, far, _, _ = bufs[stage]
        for sem in range(6):
            r_copy(stage, u, sem, far.at[u, 0], far.at[u, 0], z_next[0]).wait_send()

    def finish_first(u):
        for h, value in enumerate(finish(0, u)):
            half[u, pl.ds(4 * h, 4)] = value.reshape(4, 32, 128)
        start(1, u)

    def finish_second(u):
        values = [v.reshape(32, 128) for v in finish(1, u)]

        @pl.when(u < 8)
        def _():
            for h in (0, 1):
                left_out[u, pl.ds(32 * h, 32), :] = values[h]

        @pl.when(u >= 8)
        def _():
            for h in (0, 1):
                for m in range(4):
                    rf_out[u - 8, :, pl.ds((4 * h + m) * 128, 128)] = values[h][
                        8 * m : 8 * m + 8
                    ]

    def within(s):
        return jnp.logical_and(s >= 0, s < UNITS)

    def service(s):
        pl.when(within(s - 1))(lambda: middle(0, s - 1))
        pl.when(within(s - 2))(lambda: finish_first(s - 2))
        pl.when(within(s - 3))(lambda: middle(1, s - 3))
        pl.when(within(s - 4))(lambda: finish_second(s - 4))

    def chunk_at(u, zz, yy):
        axis = lax.rem(u, 2)
        first, second = zz + axis * (yy - zz), yy + axis * (zz - yy)
        return first * SIDE + second

    def put(ref, value):
        ref[0], ref[1] = split(value)

    def got(ref):
        return ref[0], ref[1]

    rt_load.wait()
    put(rts, rt[...])
    ct_load.wait()
    om_load.wait()
    put(cols, mm3(split(ct[...]), split(om[...]), NN).T)

    row_tile = lax.broadcasted_iota(jnp.int32, (256, 256), 0) // 64
    col_tile = lax.broadcasted_iota(jnp.int32, (256, 256), 1) // 64
    tile_ids = inner * 4 + lax.broadcasted_iota(jnp.int32, (256, 1), 0) // 64

    def left_unit(t):
        mt_copy(t).wait()
        put(ms, mt[t])
        coupling = mm3(got(ms), got(rts), NT)
        present = jnp.sum(
            (lists[pl.ds(t, 1), :] == tile_ids).astype(F32), axis=1, keepdims=True
        )
        coupling = jnp.where(row_tile == col_tile, coupling, 0.0) * present
        put(cs, coupling)
        inner_left = split(mm3(got(cols), got(cs), NT))
        lt_copy(t).wait()
        put(ls, lt[t])
        for zz in range(4):
            cut = pl.ds(256 * zz, 256)
            block = mm3(inner_left, (ls[0, :, cut], ls[1, :, cut]), NN).T
            for yy in range(4):
                part[t, chunk_at(t, zz, yy)] = block[64 * yy : 64 * yy + 64]
        start(0, t)
        projected = split(mm3(got(psts), got(ls), NT))
        put(js.at[t], mm3(projected, got(cs), NN))

    def right_unit(t):
        u = t + 8
        for n in range(4):
            cut = pl.ds(256 * n, 256)
            block = mm3(got(js.at[t]), (ws[0, :, cut], ws[1, :, cut]), NN)
            for m in (0, 1):
                value = block[:, 128 * m : 128 * m + 128].reshape(16, 8, 128)
                for i in range(16):
                    part[u, chunk_at(u, i // 4, i % 4), pl.ds((2 * n + m) * 8, 8), :] = value[i]
        start(0, u)

    def own_inverse():
        d_load.wait()
        block = dfull[target, pl.ds(pl.multiple_of(target * 128, 128), 128), :]
        rows = lax.broadcasted_iota(jnp.int32, (128, 128), 0)
        lanes = lax.broadcasted_iota(jnp.int32, (128, 128), 1)
        eye = (rows == lanes).astype(F32)
        diagonal = jnp.where(rows == lanes, block, 0.0)
        power = eye - block / jnp.sum(diagonal, axis=1, keepdims=True)
        product = eye + power
        for _ in range(6):
            power = mm_top(power, power)
            product = product + mm_top(product, power)
        dinv[target] = product / jnp.sum(diagonal, axis=0, keepdims=True)

    def solve_columns():
        for j in range(8):
            cut = pl.ds(128 * j, 128)
            rhs = ct[:, cut]
            if j > 0:
                before = pl.ds(0, 128 * j)
                rhs = rhs - mm3(
                    (ws[0, :, before], ws[1, :, before]), split(dfull[j, before, :]), NN
                )
            ws[0, :, cut], ws[1, :, cut] = split(mm3(split(rhs), split(dinv[j]), NN))

    psi_load.wait()
    put(psts, psi[...].T)

    @pl.loop(0, 8)
    def _(s):
        left_unit(s)

        @pl.when(s == 1)
        def _():
            own_inverse()
            gather_first(dinv.at[target], dinv, 8)

        @pl.when(s == 4)
        def _():
            gather_second(dfull, 0, 512)
            gather_second(dinv, 8, 64)

        @pl.when(s == 6)
        def _():
            gather_third(dfull, 0, 512)
            gather_third(dinv, 8, 64)

        service(s)

    gather_last(dfull, 0)
    gather_last(dinv, 8)
    solve_columns()

    @pl.loop(8, 16)
    def _(s):
        right_unit(s - 8)
        service(s)

    omega = split(om[...])
    for i in range(8):
        acc = jnp.zeros((128, 128), F32)
        for j in range(i, 8):
            acc += mm3(
                split(dfull[j, pl.ds(128 * i, 128), :]),
                (omega[0][128 * j : 128 * j + 128], omega[1][128 * j : 128 * j + 128]),
                NN,
            )
        doms[0, pl.ds(128 * i, 128), :], doms[1, pl.ds(128 * i, 128), :] = split(acc)

    @pl.loop(16, 20)
    def _(s):
        service(s)

    core_out[...] = mm3(
        split(rf_out[...].reshape(64, 1024)), got(doms), NN
    ).reshape(8, 8, 128)

    gather_sent(d_hbm, dfull, 0, 512)
    gather_sent(dinv, dinv, 8, 64)

    @pl.loop(0, UNITS)
    def _(u):
        sent(0, u)
        sent(1, u)


def on_device(
    left_factors, mid_factors, row_factors, col_factors, lists, sketch_right, sketch_left, diag_tile
):
    lt = jnp.swapaxes(left_factors, 2, 3).reshape(8, 256, 1024)
    mt = jnp.swapaxes(mid_factors, 2, 3).reshape(8, 256, 1024)
    rt = jnp.swapaxes(row_factors, 1, 2).reshape(256, 1024)
    ct = jnp.swapaxes(col_factors, 1, 2).reshape(256, 1024)
    hbm = pl.BlockSpec(memory_space=pl.ANY)
    vmem = pl.BlockSpec(memory_space=pltpu.VMEM)
    return pl.pallas_call(
        kernel,
        out_shape=(
            jax.ShapeDtypeStruct((8, 64, 128), F32),
            jax.ShapeDtypeStruct((8, 8, 1024), F32),
            jax.ShapeDtypeStruct((8, 8, 128), F32),
        ),
        in_specs=[hbm, hbm, hbm, hbm, vmem, hbm, hbm, hbm],
        out_specs=(vmem, vmem, vmem),
        scratch_shapes=[
            pltpu.VMEM((8, 256, 1024), F32),
            pltpu.VMEM((8, 256, 1024), F32),
            pltpu.VMEM((256, 1024), F32),
            pltpu.VMEM((256, 1024), F32),
            pltpu.VMEM((1024, 128), F32),
            pltpu.VMEM((1024, 128), F32),
            pltpu.VMEM((8, 1024, 128), F32),
            pltpu.VMEM((8, 128, 128), F32),
            pltpu.VMEM((UNITS, 16, 64, 128), F32),
            pltpu.VMEM((UNITS, 8, 32, 128), F32),
            pltpu.VMEM((UNITS, 2, 2, 64, 128), F32),
            pltpu.VMEM((UNITS, 2, 2, 2, 64, 128), F32),
            pltpu.VMEM((UNITS, 2, 1, 32, 128), F32),
            pltpu.VMEM((UNITS, 2, 2, 1, 32, 128), F32),
            pltpu.VMEM((2, 256, 1024), BF16),
            pltpu.VMEM((2, 128, 1024), BF16),
            pltpu.VMEM((2, 128, 256), BF16),
            pltpu.VMEM((2, 256, 1024), BF16),
            pltpu.VMEM((2, 256, 1024), BF16),
            pltpu.VMEM((2, 256, 256), BF16),
            pltpu.VMEM((8, 2, 128, 256), BF16),
            pltpu.VMEM((2, 256, 1024), BF16),
            pltpu.VMEM((2, 1024, 128), BF16),
            pltpu.SemaphoreType.DMA((24,)),
            pltpu.SemaphoreType.DMA((2, UNITS, 6)),
            pltpu.SemaphoreType.DMA((2, UNITS, 6)),
            pltpu.SemaphoreType.DMA((16,)),
            pltpu.SemaphoreType.DMA((16,)),
        ],
        compiler_params=pltpu.CompilerParams(
            collective_id=0, has_side_effects=True, vmem_limit_bytes=58 * 1024 * 1024
        ),
        cost_estimate=pl.CostEstimate(
            flops=6_000_000_000, bytes_accessed=21_000_000, transcendentals=0
        ),
    )(lt, mt, rt, ct, lists, sketch_right, sketch_left, diag_tile)


def solution(mesh):
    placed = (
        P("target", "inner", None, None),
        P("target", "inner", None, None),
        P("inner", None, None),
        P("inner", None, None),
        P("target", None),
        P(),
        P(),
        P(None, "target"),
    )
    return jax.shard_map(
        on_device,
        mesh=mesh,
        in_specs=placed,
        out_specs=(
            P("target", "inner", None),
            P("target", "inner", None),
            P("target", "inner", None),
        ),
        check_vma=False,
    )
```

time: 213 us -> 89.9 us (0.42); the launches traced: 209 us -> 89.6 us
  waiting for transfers between devices: 109 us -> 0 us
  Pallas kernels: 0 us -> 84.3 us
  matrix products: 62 us -> 0 us
  local copies, waits for them, and re-layouts: 20.5 us -> 4.72 us
  between operations: 16 us -> 0.64 us
    reduce_scatter x2 -> x0, waiting for transfers between devices: 108 us -> none  [the longest x1 68.4 us: on_device(): lax.psum_scatter(left_part, 'inner', scatter_dimension=1, tiled=True)]
    pallas_call x0 -> x1, Pallas kernels: none -> 84.3 us  [on_device(): pl.pallas_call(kernel, out_shape=(jax.ShapeDtypeStruct((8, 64, 128), F32)...]
    dot_general x35 -> x0, matrix products: 62 us -> none  [the longest x1 12.2 us: on_device(): jnp.einsum('tkbr,kbq->tkrq', mid_factors, row_factors, precision=precisio...]
    another operation x2 -> x0, local copies, waits for them, and re-layouts: 5.64 us -> none  [block_inverses(): jnp.stack([full_tile[j * width:(j + 1) * width, j * width:(j + 1) * width...]
    dot_general x1 -> x0, local copies, waits for them, and re-layouts: 5.39 us -> none  [on_device(): jnp.einsum('tkbr,tkrs->tbs', left_factors, inner_left, precision=precisio...]
    unnamed x20 -> x3, local copies, waits for them, and re-layouts: 7.65 us -> 4.72 us
  transfers between devices with their start and end apart: 3 -> 0, of which waited for: 2 -> 0; matrix products, arithmetic and copies ran while one was open for 39% -> 0% of each run, Pallas kernels for 0% -> 0%
where the time goes in v1:
time: 89.9 us; the launch traced here: 89.6 us
  Pallas kernels  84.3 us (94%)
  local copies, waits for them, and re-layouts  4.72 us (5%)
    pallas_call x1, Pallas kernels, on_device(): pl.pallas_call(kernel, out_shape=(jax.ShapeDtypeStruct((8, 64, 128), F32)...  84.3 us
    unnamed x3, local copies, waits for them, and re-layouts  4.72 us

profile of v1, /device:TPU:0, one launch (start us, length us, event | category | flops | bytes accessed | tf_op | source)
XLA Modules:
  0.0 89.6 jit_solution(630898107722044103)
XLA Ops:
  0.6 84.3 %shard_map.103 = (f32[8,64,128]{2,1,0:T(8,128)}, f32[8,8,1024]{2,1,0:T(8,128)}, f32[8,8,128]{2,1,0:T(8,128)}) custom-call(f32[8,256,1024]{2,1,0:T(8,128)} %bitcast.12, f32[8,256,1024]{2,1,0:T(8,128)} %bitcast.13, f32[256,1024]{1,0:T(8,128)} %bitcast.14, f32[256,1024]{1,0:T(8,128)} %bitcast.15, s32[8,64]{1,0:T(8,128)} %lists.1, f32[1024,128]{1,0:T(8,128)} %om_hbm.1, ...), custom_call_target="tpu_custom_call" | custom-call | flops 6000000000 | bytes 21000000 | tf_op jit(solution)/shard_map/pallas_call | solution.py:368
  84.9 1.7 %copy.14 = f32[8,64,128]{2,1,0:T(8,128)} copy(f32[8,64,128]{2,1,0:T(8,128)} %get-tuple-element.6) | data formatting | bytes 524288
  86.6 1.7 %copy.15 = f32[8,8,1024]{2,1,0:T(8,128)} copy(f32[8,8,1024]{2,1,0:T(8,128)} %get-tuple-element.7) | data formatting | bytes 524288
  88.2 1.4 %copy.16 = f32[8,8,128]{2,1,0:T(8,128)} copy(f32[8,8,128]{2,1,0:T(8,128)} %get-tuple-element.8) | data formatting | bytes 65536

commit v2 on v1

--- a/solution.py
+++ b/solution.py
@@ -14,6 +14,7 @@
 NT = ((1,), (1,))
 SIDE = 4
 UNITS = 16
+LAGS = (3, 6, 9, 12)
 
 
 def split(value):
@@ -39,7 +40,7 @@
     lt_hbm, mt_hbm, rt_hbm, ct_hbm, lists, om_hbm, psi_hbm, d_hbm,
     left_out, rf_out, core_out,
     lt, mt, rt, ct, om, psi, dfull, dinv, part, half, far1, near1, far2, near2,
-    rts, psts, cols, ms, ls, cs, js, ws, doms,
+    rts, psts, cols, ms, ls, cs, ws, rsf,
     in_sem, send_sem, recv_sem, gs_sem, gr_sem,
 ):
     inner = lax.axis_index("inner")
@@ -55,7 +56,19 @@
     x_next = (turn(x, 1) * 2 + core, turn(x, 3) * 2 + core)
     sibling = x * 2 + (1 - core)
 
+    barrier = pltpu.get_barrier_semaphore()
+    for peer in z_next + y_next:
+        pl.semaphore_signal(barrier, inc=1, device_id=(peer, target), device_id_type=MESH)
+    for peer in x_next + (sibling,):
+        pl.semaphore_signal(barrier, inc=1, device_id=(inner, peer), device_id_type=MESH)
+
     loads = []
+
+    def mt_copy(t):
+        return pltpu.make_async_copy(mt_hbm.at[t], mt.at[t], in_sem.at[8 + t])
+
+    def lt_copy(t):
+        return pltpu.make_async_copy(lt_hbm.at[t], lt.at[t], in_sem.at[16 + t])
 
     def load(src, dst):
         copy = pltpu.make_async_copy(src, dst, in_sem.at[len(loads)])
@@ -64,29 +77,17 @@
         return copy
 
     rt_load = load(rt_hbm, rt)
+    mt_copy(0).start()
     ct_load = load(ct_hbm, ct)
     om_load = load(om_hbm, om)
+    lt_copy(0).start()
+    psi_load = load(psi_hbm, psi)
     d_load = load(d_hbm, dfull.at[target])
-    psi_load = load(psi_hbm, psi)
-    in_base = 8
-
-    def mt_copy(t):
-        return pltpu.make_async_copy(mt_hbm.at[t], mt.at[t], in_sem.at[in_base + t])
-
-    def lt_copy(t):
-        return pltpu.make_async_copy(lt_hbm.at[t], lt.at[t], in_sem.at[in_base + 8 + t])
-
-    @pl.loop(0, 8)
+
+    @pl.loop(1, 8)
     def _(t):
         mt_copy(t).start()
         lt_copy(t).start()
-
-    barrier = pltpu.get_barrier_semaphore()
-    for peer in z_next + y_next:
-        pl.semaphore_signal(barrier, inc=1, device_id=(peer, target), device_id_type=MESH)
-    for peer in x_next + (sibling,):
-        pl.semaphore_signal(barrier, inc=1, device_id=(inner, peer), device_id_type=MESH)
-    pl.semaphore_wait(barrier, 7)
 
     def g_copy(src, dst, sem, peer):
         return pltpu.make_async_remote_copy(
@@ -129,8 +130,6 @@
         for sem in (2, 3):
             piece = dst.at[0, pl.ds(0, rows)]
             g_copy(piece, piece, base + sem, sibling).wait_send()
-
-    gather_first(d_hbm, dfull, 0)
 
     def place(u, stage):
         axis = lax.rem(u + stage, 2)
@@ -195,27 +194,26 @@
     def finish_second(u):
         values = [v.reshape(32, 128) for v in finish(1, u)]
 
+        @pl.when(u >= 8)
+        def _():
+            for h in (0, 1):
+                left_out[u - 8, pl.ds(32 * h, 32), :] = values[h]
+
         @pl.when(u < 8)
         def _():
             for h in (0, 1):
-                left_out[u, pl.ds(32 * h, 32), :] = values[h]
-
-        @pl.when(u >= 8)
-        def _():
-            for h in (0, 1):
                 for m in range(4):
-                    rf_out[u - 8, :, pl.ds((4 * h + m) * 128, 128)] = values[h][
-                        8 * m : 8 * m + 8
-                    ]
+                    rsf[u, :, pl.ds((4 * h + m) * 128, 128)] = values[h][8 * m : 8 * m + 8]
 
     def within(s):
         return jnp.logical_and(s >= 0, s < UNITS)
 
     def service(s):
-        pl.when(within(s - 1))(lambda: middle(0, s - 1))
-        pl.when(within(s - 2))(lambda: finish_first(s - 2))
-        pl.when(within(s - 3))(lambda: middle(1, s - 3))
-        pl.when(within(s - 4))(lambda: finish_second(s - 4))
+        a, b, c, d = LAGS
+        pl.when(within(s - a))(lambda: middle(0, s - a))
+        pl.when(within(s - b))(lambda: finish_first(s - b))
+        pl.when(within(s - c))(lambda: middle(1, s - c))
+        pl.when(within(s - d))(lambda: finish_second(s - d))
 
     def chunk_at(u, zz, yy):
         axis = lax.rem(u, 2)
@@ -229,46 +227,55 @@
         return ref[0], ref[1]
 
     rt_load.wait()
-    put(rts, rt[...])
+    for p in (0, 1):
+        pair = split(rt[pl.ds(128 * p, 128), :].T)
+        rts[p, :, pl.ds(0, 128)], rts[p, :, pl.ds(128, 128)] = pair
     ct_load.wait()
     om_load.wait()
-    put(cols, mm3(split(ct[...]), split(om[...]), NN).T)
-
-    row_tile = lax.broadcasted_iota(jnp.int32, (256, 256), 0) // 64
-    col_tile = lax.broadcasted_iota(jnp.int32, (256, 256), 1) // 64
-    tile_ids = inner * 4 + lax.broadcasted_iota(jnp.int32, (256, 1), 0) // 64
-
-    def left_unit(t):
+    put(ws, ct[...])
+    put(cols, mm3(got(ws), split(om[...]), NN).T)
+
+    row_tile = lax.broadcasted_iota(jnp.int32, (128, 128), 0) // 64
+    col_tile = lax.broadcasted_iota(jnp.int32, (128, 128), 1) // 64
+    tile_ids = inner * 4 + lax.broadcasted_iota(jnp.int32, (128, 1), 0) // 64
+    cs[...] = jnp.zeros_like(cs)
+
+    def right_unit(t):
         mt_copy(t).wait()
         put(ms, mt[t])
-        coupling = mm3(got(ms), got(rts), NT)
-        present = jnp.sum(
-            (lists[pl.ds(t, 1), :] == tile_ids).astype(F32), axis=1, keepdims=True
-        )
-        coupling = jnp.where(row_tile == col_tile, coupling, 0.0) * present
-        put(cs, coupling)
-        inner_left = split(mm3(got(cols), got(cs), NT))
+        for p in (0, 1):
+            cut = pl.ds(128 * p, 128)
+            both = mm(ms[0, cut, :], rts[p], NN)
+            coupling = both[:, :128] + (
+                both[:, 128:] + mm(ms[1, cut, :], rts[p, :, pl.ds(0, 128)], NN)
+            )
+            present = jnp.sum(
+                (lists[pl.ds(t, 1), :] == tile_ids + 2 * p).astype(F32), axis=1, keepdims=True
+            )
+            coupling = jnp.where(row_tile == col_tile, coupling, 0.0) * present
+            cs[t, 0, cut, cut], cs[t, 1, cut, cut] = split(coupling)
         lt_copy(t).wait()
+        put(ls, lt[t])
+        both = mm(ls[0], psts[...], NN)
+        projected = both[:, :128] + (both[:, 128:] + mm(ls[1], psts[:, pl.ds(0, 128)], NN))
+        joined = split(mm3(split(projected.T), got(cs.at[t]), NN))
+        for n in range(4):
+            cut = pl.ds(256 * n, 256)
+            block = mm3(joined, (ws[0, :, cut], ws[1, :, cut]), NN)
+            for m in (0, 1):
+                value = block[:, 128 * m : 128 * m + 128].reshape(16, 8, 128)
+                for i in range(16):
+                    part[t, chunk_at(t, i // 4, i % 4), pl.ds((2 * n + m) * 8, 8), :] = value[i]
+
+    def left_unit(t):
+        u = t + 8
+        inner_left = split(mm3(got(cols), got(cs.at[t]), NT))
         put(ls, lt[t])
         for zz in range(4):
             cut = pl.ds(256 * zz, 256)
             block = mm3(inner_left, (ls[0, :, cut], ls[1, :, cut]), NN).T
             for yy in range(4):
-                part[t, chunk_at(t, zz, yy)] = block[64 * yy : 64 * yy + 64]
-        start(0, t)
-        projected = split(mm3(got(psts), got(ls), NT))
-        put(js.at[t], mm3(projected, got(cs), NN))
-
-    def right_unit(t):
-        u = t + 8
-        for n in range(4):
-            cut = pl.ds(256 * n, 256)
-            block = mm3(got(js.at[t]), (ws[0, :, cut], ws[1, :, cut]), NN)
-            for m in (0, 1):
-                value = block[:, 128 * m : 128 * m + 128].reshape(16, 8, 128)
-                for i in range(16):
-                    part[u, chunk_at(u, i // 4, i % 4), pl.ds((2 * n + m) * 8, 8), :] = value[i]
-        start(0, u)
+                part[u, chunk_at(u, zz, yy)] = block[64 * yy : 64 * yy + 64]
 
     def own_inverse():
         d_load.wait()
@@ -284,68 +291,69 @@
             product = product + mm_top(product, power)
         dinv[target] = product / jnp.sum(diagonal, axis=0, keepdims=True)
 
-    def solve_columns():
-        for j in range(8):
-            cut = pl.ds(128 * j, 128)
-            rhs = ct[:, cut]
-            if j > 0:
-                before = pl.ds(0, 128 * j)
-                rhs = rhs - mm3(
-                    (ws[0, :, before], ws[1, :, before]), split(dfull[j, before, :]), NN
-                )
-            ws[0, :, cut], ws[1, :, cut] = split(mm3(split(rhs), split(dinv[j]), NN))
+    def solve_step(j):
+        cut = pl.ds(128 * j, 128)
+        rhs = rsf[:, :, cut].reshape(64, 128)
+        if j > 0:
+            before = pl.ds(0, 128 * j)
+            earlier = rf_out[:, :, before].reshape(64, 128 * j)
+            rhs = rhs - mm3(split(earlier), split(dfull[j, before, :]), NN)
+        rf_out[:, :, cut] = mm3(split(rhs), split(dinv[j]), NN).reshape(8, 8, 128)
 
     psi_load.wait()
-    put(psts, psi[...].T)
-
-    @pl.loop(0, 8)
+    psts[:, pl.ds(0, 128)], psts[:, pl.ds(128, 128)] = split(psi[...])
+    right_unit(0)
+    pl.semaphore_wait(barrier, 7)
+    start(0, 0)
+    gather_first(d_hbm, dfull, 0)
+
+    @pl.loop(1, 8)
     def _(s):
-        left_unit(s)
-
-        @pl.when(s == 1)
-        def _():
-            own_inverse()
-            gather_first(dinv.at[target], dinv, 8)
-
-        @pl.when(s == 4)
+        right_unit(s)
+        start(0, s)
+        service(s)
+
+    @pl.loop(8, 16)
+    def _(s):
+        left_unit(s - 8)
+        start(0, s)
+
+        @pl.when(s == 12)
         def _():
             gather_second(dfull, 0, 512)
+
+        service(s)
+
+    own_inverse()
+    gather_first(dinv.at[target], dinv, 8)
+    gather_third(dfull, 0, 512)
+    solve_from = max(16, 8 + LAGS[3])
+
+    @pl.loop(16, solve_from)
+    def _(s):
+        service(s)
+
+        @pl.when(s == 17)
+        def _():
             gather_second(dinv, 8, 64)
 
-        @pl.when(s == 6)
+        @pl.when(s == 18)
         def _():
-            gather_third(dfull, 0, 512)
             gather_third(dinv, 8, 64)
-
-        service(s)
 
     gather_last(dfull, 0)
     gather_last(dinv, 8)
-    solve_columns()
-
-    @pl.loop(8, 16)
-    def _(s):
-        right_unit(s - 8)
-        service(s)
-
-    omega = split(om[...])
-    for i in range(8):
-        acc = jnp.zeros((128, 128), F32)
-        for j in range(i, 8):
-            acc += mm3(
-                split(dfull[j, pl.ds(128 * i, 128), :]),
-                (omega[0][128 * j : 128 * j + 128], omega[1][128 * j : 128 * j + 128]),
-                NN,
-            )
-        doms[0, pl.ds(128 * i, 128), :], doms[1, pl.ds(128 * i, 128), :] = split(acc)
-
-    @pl.loop(16, 20)
+    for j in range(8):
+        solve_step(j)
+        if j % 2:
+            service(solve_from + j // 2)
+    core_out[...] = mm3(
+        split(rsf[...].reshape(64, 1024)), split(om[...]), NN
+    ).reshape(8, 8, 128)
+
+    @pl.loop(solve_from + 4, 16 + LAGS[3])
     def _(s):
         service(s)
-
-    core_out[...] = mm3(
-        split(rf_out[...].reshape(64, 1024)), got(doms), NN
-    ).reshape(8, 8, 128)
 
     gather_sent(d_hbm, dfull, 0, 512)
     gather_sent(dinv, dinv, 8, 64)
@@ -354,6 +362,12 @@
     def _(u):
         sent(0, u)
         sent(1, u)
+
+
+def hand_over(a, b, c, a_out, b_out, c_out):
+    a_out[...] = a[...]
+    b_out[...] = b[...]
+    c_out[...] = c[...]
 
 
 def on_device(
@@ -365,7 +379,7 @@
     ct = jnp.swapaxes(col_factors, 1, 2).reshape(256, 1024)
     hbm = pl.BlockSpec(memory_space=pl.ANY)
     vmem = pl.BlockSpec(memory_space=pltpu.VMEM)
-    return pl.pallas_call(
+    parts = pl.pallas_call(
         kernel,
         out_shape=(
             jax.ShapeDtypeStruct((8, 64, 128), F32),
@@ -389,15 +403,14 @@
             pltpu.VMEM((UNITS, 2, 2, 2, 64, 128), F32),
             pltpu.VMEM((UNITS, 2, 1, 32, 128), F32),
             pltpu.VMEM((UNITS, 2, 2, 1, 32, 128), F32),
-            pltpu.VMEM((2, 256, 1024), BF16),
-            pltpu.VMEM((2, 128, 1024), BF16),
+            pltpu.VMEM((2, 1024, 256), BF16),
+            pltpu.VMEM((1024, 256), BF16),
             pltpu.VMEM((2, 128, 256), BF16),
             pltpu.VMEM((2, 256, 1024), BF16),
             pltpu.VMEM((2, 256, 1024), BF16),
-            pltpu.VMEM((2, 256, 256), BF16),
-            pltpu.VMEM((8, 2, 128, 256), BF16),
+            pltpu.VMEM((8, 2, 256, 256), BF16),
             pltpu.VMEM((2, 256, 1024), BF16),
-            pltpu.VMEM((2, 1024, 128), BF16),
+            pltpu.VMEM((8, 8, 1024), F32),
             pltpu.SemaphoreType.DMA((24,)),
             pltpu.SemaphoreType.DMA((2, UNITS, 6)),
             pltpu.SemaphoreType.DMA((2, UNITS, 6)),
@@ -411,6 +424,13 @@
             flops=6_000_000_000, bytes_accessed=21_000_000, transcendentals=0
         ),
     )(lt, mt, rt, ct, lists, sketch_right, sketch_left, diag_tile)
+    return pl.pallas_call(
+        hand_over,
+        out_shape=tuple(jax.ShapeDtypeStruct(p.shape, F32) for p in parts),
+        in_specs=[vmem] * 3,
+        out_specs=(vmem,) * 3,
+        cost_estimate=pl.CostEstimate(flops=0, bytes_accessed=1_200_000, transcendentals=0),
+    )(*parts)
 
 
 def solution(mesh):

time: 89.9 us -> 67.4 us (0.75)
  Pallas kernels: 84.3 us -> 65.8 us
  local copies, waits for them, and re-layouts: 4.72 us -> 0 us
    pallas_call x1, Pallas kernels: 84.3 us -> 64 us  [on_device(): pl.pallas_call(kernel, out_shape=(jax.ShapeDtypeStruct((8, 64, 128), F32)...]
    unnamed x3 -> x0, local copies, waits for them, and re-layouts: 4.72 us -> none
    pallas_call x0 -> x1, Pallas kernels: none -> 1.84 us  [on_device(): pl.pallas_call(hand_over, out_shape=tuple((jax.ShapeDtypeStruct(p.shape,...]
where the time goes in v2:
time: 67.4 us; the launch traced here: 66.5 us
  Pallas kernels  65.8 us (98%)
    pallas_call x1, Pallas kernels, on_device(): pl.pallas_call(kernel, out_shape=(jax.ShapeDtypeStruct((8, 64, 128), F32)...  64 us
    pallas_call x1, Pallas kernels, on_device(): pl.pallas_call(hand_over, out_shape=tuple((jax.ShapeDtypeStruct(p.shape,...  1.84 us

profile of v2, /device:TPU:0, one launch (start us, length us, event | category | flops | bytes accessed | tf_op | source)
XLA Modules:
  0.0 66.5 jit_solution(3330072602772856801)
XLA Ops:
  0.6 64.0 %shard_map.103 = (f32[8,64,128]{2,1,0:T(8,128)}, f32[8,8,1024]{2,1,0:T(8,128)}, f32[8,8,128]{2,1,0:T(8,128)}) custom-call(f32[8,256,1024]{2,1,0:T(8,128)} %bitcast.12, f32[8,256,1024]{2,1,0:T(8,128)} %bitcast.13, f32[256,1024]{1,0:T(8,128)} %bitcast.14, f32[256,1024]{1,0:T(8,128)} %bitcast.15, s32[8,64]{1,0:T(8,128)} %lists.1, f32[1024,128]{1,0:T(8,128)} %om_hbm.1, ...), custom_call_target="tpu_custom_call" | custom-call | flops 6000000000 | bytes 21000000 | tf_op jit(solution)/shard_map/pallas_call | solution.py:382
  64.6 1.8 %shard_map.104 = (f32[8,64,128]{2,1,0:T(8,128)}, f32[8,8,1024]{2,1,0:T(8,128)}, f32[8,8,128]{2,1,0:T(8,128)}) custom-call(f32[8,64,128]{2,1,0:T(8,128)} %get-tuple-element.6.a, f32[8,8,1024]{2,1,0:T(8,128)} %get-tuple-element.7.b, f32[8,8,128]{2,1,0:T(8,128)} %get-tuple-element.8.c), custom_call_target="tpu_custom_call" | custom-call | bytes 1200000 | tf_op jit(solution)/shard_map/pallas_call | solution.py:427

commit v3 on v2

--- a/solution.py
+++ b/solution.py
@@ -142,7 +142,7 @@
     def r_copy(stage, u, sem, src, dst, peer):
         return pltpu.make_async_remote_copy(
             src_ref=src, dst_ref=dst,
-            send_sem=send_sem.at[stage, u, sem], recv_sem=recv_sem.at[stage, u, sem],
+            send_sem=send_sem.at[stage, min(sem // 2, 1)], recv_sem=recv_sem.at[stage, u, sem],
             device_id=(peer, target), device_id_type=MESH,
         )
 
@@ -181,10 +181,10 @@
             piece(stage, u, pos, h)[...] + near[u, 0, h] + near[u, 1, h] for h in (0, 1)
         ]
 
-    def sent(stage, u):
-        _, far, _, _ = bufs[stage]
-        for sem in range(6):
-            r_copy(stage, u, sem, far.at[u, 0], far.at[u, 0], z_next[0]).wait_send()
+    def sent(stage):
+        _, far, near, _ = bufs[stage]
+        r_copy(stage, 0, 0, far, far, z_next[0]).wait_send()
+        r_copy(stage, 0, 2, near, near, z_next[0]).wait_send()
 
     def finish_first(u):
         for h, value in enumerate(finish(0, u)):
@@ -318,28 +318,28 @@
         left_unit(s - 8)
         start(0, s)
 
+        @pl.when(s == 9)
+        def _():
+            own_inverse()
+            gather_first(dinv.at[target], dinv, 8)
+
         @pl.when(s == 12)
         def _():
             gather_second(dfull, 0, 512)
+            gather_second(dinv, 8, 64)
+
+        @pl.when(s == 15)
+        def _():
+            gather_third(dfull, 0, 512)
+            gather_third(dinv, 8, 64)
 
         service(s)
 
-    own_inverse()
-    gather_first(dinv.at[target], dinv, 8)
-    gather_third(dfull, 0, 512)
     solve_from = max(16, 8 + LAGS[3])
 
     @pl.loop(16, solve_from)
     def _(s):
         service(s)
-
-        @pl.when(s == 17)
-        def _():
-            gather_second(dinv, 8, 64)
-
-        @pl.when(s == 18)
-        def _():
-            gather_third(dinv, 8, 64)
 
     gather_last(dfull, 0)
     gather_last(dinv, 8)
@@ -358,10 +358,8 @@
     gather_sent(d_hbm, dfull, 0, 512)
     gather_sent(dinv, dinv, 8, 64)
 
-    @pl.loop(0, UNITS)
-    def _(u):
-        sent(0, u)
-        sent(1, u)
+    sent(0)
+    sent(1)
 
 
 def hand_over(a, b, c, a_out, b_out, c_out):
@@ -412,7 +410,7 @@
             pltpu.VMEM((2, 256, 1024), BF16),
             pltpu.VMEM((8, 8, 1024), F32),
             pltpu.SemaphoreType.DMA((24,)),
-            pltpu.SemaphoreType.DMA((2, UNITS, 6)),
+            pltpu.SemaphoreType.DMA((2, 2)),
             pltpu.SemaphoreType.DMA((2, UNITS, 6)),
             pltpu.SemaphoreType.DMA((16,)),
             pltpu.SemaphoreType.DMA((16,)),

time: 67.4 us -> 64.9 us (0.963); the launches traced: 66.5 us -> 64.8 us
  Pallas kernels: 65.8 us -> 64.1 us
    pallas_call x1, Pallas kernels: 64 us -> 62.3 us  [on_device(): pl.pallas_call(kernel, out_shape=(jax.ShapeDtypeStruct((8, 64, 128), F32)...]
where the time goes in v3:
time: 64.9 us; the launch traced here: 64.8 us
  Pallas kernels  64.1 us (99%)
    pallas_call x1, Pallas kernels, on_device(): pl.pallas_call(kernel, out_shape=(jax.ShapeDtypeStruct((8, 64, 128), F32)...  62.3 us
    pallas_call x1, Pallas kernels, on_device(): pl.pallas_call(hand_over, out_shape=tuple((jax.ShapeDtypeStruct(p.shape,...  1.84 us

profile of v3, /device:TPU:0, one launch (start us, length us, event | category | flops | bytes accessed | tf_op | source)
XLA Modules:
  0.0 64.8 jit_solution(6966595534240736468)
XLA Ops:
  0.6 62.3 %shard_map.103 = (f32[8,64,128]{2,1,0:T(8,128)}, f32[8,8,1024]{2,1,0:T(8,128)}, f32[8,8,128]{2,1,0:T(8,128)}) custom-call(f32[8,256,1024]{2,1,0:T(8,128)} %bitcast.12, f32[8,256,1024]{2,1,0:T(8,128)} %bitcast.13, f32[256,1024]{1,0:T(8,128)} %bitcast.14, f32[256,1024]{1,0:T(8,128)} %bitcast.15, s32[8,64]{1,0:T(8,128)} %lists.1, f32[1024,128]{1,0:T(8,128)} %om_hbm.1, ...), custom_call_target="tpu_custom_call" | custom-call | flops 6000000000 | bytes 21000000 | tf_op jit(solution)/shard_map/pallas_call | solution.py:380
  62.9 1.8 %shard_map.104 = (f32[8,64,128]{2,1,0:T(8,128)}, f32[8,8,1024]{2,1,0:T(8,128)}, f32[8,8,128]{2,1,0:T(8,128)}) custom-call(f32[8,64,128]{2,1,0:T(8,128)} %get-tuple-element.6.a, f32[8,8,1024]{2,1,0:T(8,128)} %get-tuple-element.7.b, f32[8,8,128]{2,1,0:T(8,128)} %get-tuple-element.8.c), custom_call_target="tpu_custom_call" | custom-call | bytes 1200000 | tf_op jit(solution)/shard_map/pallas_call | solution.py:425

commit v4 on v3

--- a/solution.py
+++ b/solution.py
@@ -142,7 +142,7 @@
     def r_copy(stage, u, sem, src, dst, peer):
         return pltpu.make_async_remote_copy(
             src_ref=src, dst_ref=dst,
-            send_sem=send_sem.at[stage, min(sem // 2, 1)], recv_sem=recv_sem.at[stage, u, sem],
+            send_sem=send_sem.at[stage, min(sem // 2, 1)], recv_sem=recv_sem.at[stage, u, min(sem // 2, 1)],
             device_id=(peer, target), device_id_type=MESH,
         )
 
@@ -164,19 +164,16 @@
     def middle(stage, u):
         pos, peers = place(u, stage)
         _, far, near, _ = bufs[stage]
+        r_copy(stage, u, 0, far.at[u], far.at[u], peers[0]).wait_recv()
         for d in (0, 1):
             own = piece(stage, u, turn(pos, 1 + 2 * d), d)
-            r_copy(stage, u, d, far.at[u, d], far.at[u, d], peers[d]).wait_recv()
             own[...] += far[u, d]
             r_copy(stage, u, 4 + d, own, near.at[u, d, d], peers[d]).start()
 
     def finish(stage, u):
         pos, peers = place(u, stage)
         _, far, near, _ = bufs[stage]
-        for d in (0, 1):
-            for h in (0, 1):
-                sem = 4 + d if h == d else 2 + d
-                r_copy(stage, u, sem, near.at[u, d, h], near.at[u, d, h], peers[d]).wait_recv()
+        r_copy(stage, u, 2, near.at[u], near.at[u], peers[0]).wait_recv()
         return [
             piece(stage, u, pos, h)[...] + near[u, 0, h] + near[u, 1, h] for h in (0, 1)
         ]
@@ -411,7 +408,7 @@
             pltpu.VMEM((8, 8, 1024), F32),
             pltpu.SemaphoreType.DMA((24,)),
             pltpu.SemaphoreType.DMA((2, 2)),
-            pltpu.SemaphoreType.DMA((2, UNITS, 6)),
+            pltpu.SemaphoreType.DMA((2, UNITS, 2)),
             pltpu.SemaphoreType.DMA((16,)),
             pltpu.SemaphoreType.DMA((16,)),
         ],

time: 64.9 us -> 63.7 us (0.982)
  Pallas kernels: 64.1 us -> 62.9 us
    pallas_call x1, Pallas kernels: 62.3 us -> 61.1 us  [on_device(): pl.pallas_call(kernel, out_shape=(jax.ShapeDtypeStruct((8, 64, 128), F32)...]
where the time goes in v4:
time: 63.7 us; the launch traced here: 63.6 us
  Pallas kernels  62.9 us (99%)
  between operations  0.64 us (1%)
    pallas_call x1, Pallas kernels, on_device(): pl.pallas_call(kernel, out_shape=(jax.ShapeDtypeStruct((8, 64, 128), F32)...  61.1 us
    pallas_call x1, Pallas kernels, on_device(): pl.pallas_call(hand_over, out_shape=tuple((jax.ShapeDtypeStruct(p.shape,...  1.84 us

profile of v4, /device:TPU:0, one launch (start us, length us, event | category | flops | bytes accessed | tf_op | source)
XLA Modules:
  0.0 63.6 jit_solution(10841425584980294703)
XLA Ops:
  0.6 61.1 %shard_map.103 = (f32[8,64,128]{2,1,0:T(8,128)}, f32[8,8,1024]{2,1,0:T(8,128)}, f32[8,8,128]{2,1,0:T(8,128)}) custom-call(f32[8,256,1024]{2,1,0:T(8,128)} %bitcast.12, f32[8,256,1024]{2,1,0:T(8,128)} %bitcast.13, f32[256,1024]{1,0:T(8,128)} %bitcast.14, f32[256,1024]{1,0:T(8,128)} %bitcast.15, s32[8,64]{1,0:T(8,128)} %lists.1, f32[1024,128]{1,0:T(8,128)} %om_hbm.1, ...), custom_call_target="tpu_custom_call" | custom-call | flops 6000000000 | bytes 21000000 | tf_op jit(solution)/shard_map/pallas_call | solution.py:377
  61.7 1.8 %shard_map.104 = (f32[8,64,128]{2,1,0:T(8,128)}, f32[8,8,1024]{2,1,0:T(8,128)}, f32[8,8,128]{2,1,0:T(8,128)}) custom-call(f32[8,64,128]{2,1,0:T(8,128)} %get-tuple-element.6.a, f32[8,8,1024]{2,1,0:T(8,128)} %get-tuple-element.7.b, f32[8,8,128]{2,1,0:T(8,128)} %get-tuple-element.8.c), custom_call_target="tpu_custom_call" | custom-call | bytes 1200000 | tf_op jit(solution)/shard_map/pallas_call | solution.py:422

commit v5 on v4

--- a/solution.py
+++ b/solution.py
@@ -155,7 +155,7 @@
         _, far, near, _ = bufs[stage]
         for d in (0, 1):
             r_copy(stage, u, d, piece(stage, u, turn(pos, 2), d), far.at[u, d], peers[d]).start()
-        for d in (0, 1):
+        for d in (0, 1) if stage == 0 else ():
             r_copy(
                 stage, u, 2 + d, piece(stage, u, turn(pos, 1 + 2 * d), 1 - d),
                 near.at[u, d, 1 - d], peers[d],
@@ -168,7 +168,11 @@
         for d in (0, 1):
             own = piece(stage, u, turn(pos, 1 + 2 * d), d)
             own[...] += far[u, d]
-            r_copy(stage, u, 4 + d, own, near.at[u, d, d], peers[d]).start()
+            if stage == 0:
+                r_copy(stage, u, 4 + d, own, near.at[u, d, d], peers[d]).start()
+            else:
+                both = half.at[u, pl.ds(2 * turn(pos, 1 + 2 * d), 2)]
+                r_copy(stage, u, 4 + d, both, near.at[u, d, :, 0], peers[d]).start()
 
     def finish(stage, u):
         pos, peers = place(u, stage)

time: 63.7 us -> 63.4 us (level)
  no operation moved by 1% of the time
where the time goes in v5:
time: 63.4 us; the launch traced here: 63.3 us
  Pallas kernels  62.6 us (99%)
  between operations  0.64 us (1%)
    pallas_call x1, Pallas kernels, on_device(): pl.pallas_call(kernel, out_shape=(jax.ShapeDtypeStruct((8, 64, 128), F32)...  60.8 us
    pallas_call x1, Pallas kernels, on_device(): pl.pallas_call(hand_over, out_shape=tuple((jax.ShapeDtypeStruct(p.shape,...  1.84 us

profile of v5, /device:TPU:0, one launch (start us, length us, event | category | flops | bytes accessed | tf_op | source)
XLA Modules:
  0.0 63.3 jit_solution(14662222813508249138)
XLA Ops:
  0.6 60.8 %shard_map.103 = (f32[8,64,128]{2,1,0:T(8,128)}, f32[8,8,1024]{2,1,0:T(8,128)}, f32[8,8,128]{2,1,0:T(8,128)}) custom-call(f32[8,256,1024]{2,1,0:T(8,128)} %bitcast.12, f32[8,256,1024]{2,1,0:T(8,128)} %bitcast.13, f32[256,1024]{1,0:T(8,128)} %bitcast.14, f32[256,1024]{1,0:T(8,128)} %bitcast.15, s32[8,64]{1,0:T(8,128)} %lists.1, f32[1024,128]{1,0:T(8,128)} %om_hbm.1, ...), custom_call_target="tpu_custom_call" | custom-call | flops 6000000000 | bytes 21000000 | tf_op jit(solution)/shard_map/pallas_call | solution.py:381
  61.4 1.8 %shard_map.104 = (f32[8,64,128]{2,1,0:T(8,128)}, f32[8,8,1024]{2,1,0:T(8,128)}, f32[8,8,128]{2,1,0:T(8,128)}) custom-call(f32[8,64,128]{2,1,0:T(8,128)} %get-tuple-element.6.a, f32[8,8,1024]{2,1,0:T(8,128)} %get-tuple-element.7.b, f32[8,8,128]{2,1,0:T(8,128)} %get-tuple-element.8.c), custom_call_target="tpu_custom_call" | custom-call | bytes 1200000 | tf_op jit(solution)/shard_map/pallas_call | solution.py:426
